TPU v7x, 256 devices: a whole 4x4x8 slice. The times are simulated.
256 devices in a mesh: sec: 4 (over x), ch: 64 (over y, z, core).
Axes of the slice: x: 4, y: 4, z: 8, core: 2. Of those that a mesh axis runs over, the one named last changes fastest.
Arguments:
- strain_rate: bfloat16 [4, 32768, 4156], P(None, ('sec', 'ch')), may hold values from -60 to 60
- fir_taps: bfloat16 [64], replicated, may hold values from -0.75 to 0.75
- gain_code: int32 [32768], P(('sec', 'ch')), may hold values from 1 to 8
- alive_mask: int32 [32768], P(('sec', 'ch')), may hold values 0 or 1
- band_low: int32 [1], replicated, may hold values from 1 to 255
- band_high: int32 [1], replicated, may hold values from 256 to 510
- slow_limit: int32 [1], replicated, may hold values from 200 to 599
- fast_limit: int32 [1], replicated, may hold values from 1500 to 4999
Outputs:
- filtered: float32 [4, 32768, 1024], P('sec', 'ch')
All inputs are finite; a program needn't handle non-finite values. No bound on the sum of `alive_mask` on one device may be relied on, other than what follows from the above.
Results may differ from a plain program's by a relative error of at most 0.0003.
Values sent between devices are 32-bit elements; how exact they have to be, the bound alone decides.
A program may use at most 128 MiB of HBM per device.

v0:
```python
import math

import jax
import jax.numpy as jnp
from jax import lax
from jax.sharding import PartitionSpec as P

TAPS = 64
DECIM = 4
SMOOTH = 4


FLOOR = 0.05
TOP_FREQUENCY = lax.Precision.HIGHEST


def complex_table(phase, period, sign):
    angle = phase.astype(jnp.float32) * (sign * 2.0 * math.pi / period)
    cosine = jnp.cos(angle)
    sine = jnp.sin(angle)
    return jnp.stack(
        [jnp.stack([cosine, -sine], axis=1), jnp.stack([sine, cosine], axis=1)], axis=0
    )


def rotate(field, phase, period, sign):
    angle = phase.astype(jnp.float32) * (sign * 2.0 * math.pi / period)
    cosine = jnp.cos(angle)
    sine = jnp.sin(angle)
    real_part = field[:, :, 0]
    imag_part = field[:, :, 1]
    return jnp.stack(
        [cosine * real_part - sine * imag_part, sine * real_part + cosine * imag_part], axis=2
    )


def time_tables(samples, bins):
    times = jnp.arange(samples, dtype=jnp.int32)
    frequencies = jnp.arange(bins, dtype=jnp.int32)
    phase = times[:, None] * frequencies[None, :] % samples
    angle = phase.astype(jnp.float32) * (2.0 * math.pi / samples)
    scaling = 1.0 / math.sqrt(samples)
    cosine = jnp.cos(angle)
    sine = jnp.sin(angle)
    forward_transform = jnp.stack([cosine * scaling, -sine * scaling], axis=1)
    backward = jnp.stack([cosine.T, -sine.T], axis=0) * (2.0 * scaling)
    return (forward_transform, backward)


def fir_tables(fir_taps):
    span = DECIM * 128
    outputs = jnp.arange(128, dtype=jnp.int32)
    offsets = jnp.arange(TAPS, dtype=jnp.int32)
    main_lead = jnp.arange(span, dtype=jnp.int32)[:, None] - DECIM * outputs[None, :]
    tail_lead = span + jnp.arange(TAPS - DECIM, dtype=jnp.int32)[:, None] - DECIM * outputs[None, :]
    main_onehot = (main_lead[:, :, None] == offsets).astype(jnp.bfloat16)
    tail_onehot = (tail_lead[:, :, None] == offsets).astype(jnp.bfloat16)
    main_table = jnp.einsum(
        "iok,k->io", main_onehot, fir_taps, preferred_element_type=jnp.float32
    ).astype(jnp.bfloat16)
    tail_table = jnp.einsum(
        "iok,k->io", tail_onehot, fir_taps, preferred_element_type=jnp.float32
    ).astype(jnp.bfloat16)
    return (main_table, tail_table)


def decimate(strain, main_table, tail_table):
    windows, channels, length = strain.shape
    span = DECIM * 128
    blocks = (length - (TAPS - DECIM)) // span
    main_part = strain[:, :, : blocks * span].reshape(windows, channels, blocks, span)
    following = jnp.concatenate(
        [main_part[:, :, 1:, : TAPS - DECIM], strain[:, :, None, blocks * span :]], axis=2
    )
    total = jnp.einsum("wcbi,io->wcbo", main_part, main_table, preferred_element_type=jnp.float32)
    total = total + jnp.einsum(
        "wcbi,io->wcbo", following, tail_table, preferred_element_type=jnp.float32
    )
    return total.reshape(windows, channels, blocks * 128)


def whiten(frequency_content, weight, band):
    real_part = frequency_content[:, :, 0]
    imag_part = frequency_content[:, :, 1]
    amplitude = jnp.sqrt(real_part * real_part + imag_part * imag_part)
    width = amplitude.shape[1]
    padded = jnp.pad(amplitude, ((0, 0), (SMOOTH, SMOOTH), (0, 0)))
    total = padded[:, 0:width]
    for shift in range(1, 2 * SMOOTH + 1):
        total = total + padded[:, shift : shift + width]
    smooth = total / (2 * SMOOTH + 1)
    factor = band[None, :, None] * weight[None, None, :] / jnp.maximum(smooth, FLOOR)
    return frequency_content * factor[:, :, None, :]


def per_device(
    strain_rate, fir_taps, gain_code, alive_mask, band_low, band_high, slow_limit, fast_limit
):
    sections = lax.axis_size("sec")
    shards = lax.axis_size("ch")
    windows, channels, length = strain_rate.shape
    samples = (length - TAPS + DECIM) // DECIM
    bins = samples // 2
    main_table, tail_table = fir_tables(fir_taps)
    downsampled_traces = decimate(strain_rate, main_table, tail_table)
    forward_transform, backward = time_tables(samples, bins)
    frequency_content = jnp.einsum(
        "eqy,ynm->emnq", downsampled_traces, forward_transform, precision=TOP_FREQUENCY
    )
    bin_index = jnp.arange(bins, dtype=jnp.int32)
    band = ((bin_index >= band_low[0]) & (bin_index <= band_high[0])).astype(jnp.float32)
    weight = gain_code.astype(jnp.float32) * 0.25 * alive_mask.astype(jnp.float32)
    whitened = whiten(frequency_content, weight, band)
    traces = jnp.einsum("wfrc,rft->wct", whitened, backward, precision=TOP_FREQUENCY)
    received_traces = lax.all_to_all(traces, "sec", split_axis=0, concat_axis=1, tiled=True)
    repeated_pass = jnp.einsum(
        "eqy,ynm->emnq", received_traces, forward_transform, precision=TOP_FREQUENCY
    )
    by_bins = lax.all_to_all(repeated_pass, "ch", split_axis=1, concat_axis=3, tiled=True)
    groups = by_bins.shape[0]
    local_bins = by_bins.shape[1]
    block_count = sections * shards
    total_channels = block_count * channels
    arranged = by_bins.reshape(groups, local_bins, 2, shards, sections, channels)
    wave_index = jnp.arange(block_count, dtype=jnp.int32)
    shard_index = jnp.arange(shards, dtype=jnp.int32)
    section_index = jnp.arange(sections, dtype=jnp.int32)
    block_number = section_index[None, :] * shards + shard_index[:, None]
    outer_table = complex_table(
        wave_index[:, None, None] * block_number[None] % block_count, block_count, -1.0
    )
    segment_one = jnp.einsum("okrcs,gfrcsj->gfokj", outer_table, arranged, precision=TOP_FREQUENCY)
    trace_index = jnp.arange(channels, dtype=jnp.int32)
    twist = wave_index[:, None] * trace_index[None, :] % total_channels
    segment_one = rotate(segment_one, twist, total_channels, -1.0)
    inner_phase = trace_index[:, None] * trace_index[None, :] % channels
    inner_table = complex_table(inner_phase, channels, -1.0)
    wavefield = jnp.einsum("oarj,gfrkj->gfoka", inner_table, segment_one, precision=TOP_FREQUENCY)
    wavenumber = wave_index[:, None] + block_count * trace_index[None, :]
    channel_spacing = jnp.minimum(wavenumber, total_channels - wavenumber)
    rate = 500 * total_channels // samples
    bin_global = lax.axis_index("ch") * local_bins + jnp.arange(local_bins, dtype=jnp.int32)
    reach = bin_global * rate
    fan = (
        (slow_limit[0] * channel_spacing[None, :, :] <= reach[:, None, None])
        & (reach[:, None, None] <= fast_limit[0] * channel_spacing[None, :, :])
    ).astype(jnp.float32)
    wavefield = wavefield * fan[None, :, None, :, :]
    inner_back = complex_table(inner_phase, channels, 1.0)
    segment_two = jnp.einsum("ojra,gfrka->gfokj", inner_back, wavefield, precision=TOP_FREQUENCY)
    segment_two = rotate(segment_two, twist, total_channels, 1.0)
    outer_back = complex_table(
        wave_index[:, None] * wave_index[None, :] % block_count, block_count, 1.0
    )
    passed = jnp.einsum("obrk,gfrkj->gfobj", outer_back, segment_two, precision=TOP_FREQUENCY) * (
        1.0 / total_channels
    )
    passed = passed.reshape(groups, local_bins, 2, total_channels)
    returned = lax.all_to_all(passed, "ch", split_axis=3, concat_axis=1, tiled=True)
    return jnp.einsum("gfrc,rft->gct", returned, backward, precision=TOP_FREQUENCY)


def solution(mesh):
    placed = (
        P(None, ("sec", "ch"), None),
        P(),
        P(("sec", "ch")),
        P(("sec", "ch")),
        P(),
        P(),
        P(),
        P(),
    )
    return jax.shard_map(
        per_device, mesh=mesh, in_specs=placed, out_specs=P("sec", "ch", None), check_vma=False
    )
```

profile of v0, /device:TPU:1, one launch (start us, length us, event | category | flops | bytes accessed | tf_op | source)
XLA Modules:
  0.0 437.0 jit_solution(12544947026307717471)
XLA Ops:
  0.0 9.2 %negate_multiply_fusion = (f32[1024,1,512]{0,2,1:T(8,128)S(1)}, f32[1024,1,512]{0,2,1:T(8,128)}) fusion(), kind=kLoop, calls=%fused_computation.47 | loop fusion | flops 8912896 | bytes 4194304 | tf_op jit(solution)/shard_map/mul | solution.py:45
  9.2 9.6 %sine_negate_fusion = (f32[1,512,1024]{2,1,0:T(8,128)}, f32[1,512,1024]{2,1,0:T(8,128)}) fusion(), kind=kLoop, calls=%fused_computation.43 | loop fusion | flops 7864320 | bytes 4194304 | tf_op jit(solution)/shard_map/neg | solution.py:46
  18.8 0.5 copy.139
  19.3 2.0 copy-done.6
  21.5 0.4 fusion.35
  21.9 2.6 fusion
  24.6 0.5 fusion.67
  25.1 3.1 bitcast_add_fusion
  28.3 6.7 %fusion.43 = f32[4,512,2,128]{3,1,0,2:T(8,128)S(1)} fusion(f32[4,128,1024,1]{1,2,0,3:T(8,128)S(1)} %bitcast.186, f32[1024,1,512]{0,2,1:T(8,128)S(1)} %get-tuple-element.22, f32[1024,1,512]{0,2,1:T(8,128)S(1)} %copy-done.2), kind=kOutput, calls=%fused_computation.58 | convolution fusion | flops 6443499520 | bytes 8388608 | tf_op jit(solution)/shard_map/eqy,ynm->emnq/dot_general | solution.py:107
  35.0 0.3 fusion.56
  37.1 0.9 maximum_divide_fusion
  38.0 18.2 %fusion.46 = f32[4,128,1024]{2,1,0:T(8,128)S(1)} fusion(f32[1,512,1024]{2,1,0:T(8,128)S(1)} %copy-done.3, f32[1,512,1024]{2,1,0:T(8,128)S(1)} %copy-done.5, f32[4,512,2,128]{3,1,0,2:T(8,128)S(1)} %fusion.43, f32[4,512,128]{2,1,0:T(8,128)S(1)} %maximum_divide_fusion), kind=kOutput, calls=%fused_computation.59 | convolution fusion | flops 6445072384 | bytes 9437184 | tf_op jit(solution)/shard_map/wfrc,rft->wct/dot_general | solution.py:114
  56.2 29.9 %all_to_all.39 = f32[4,128,1024]{2,1,0:T(8,128)S(1)} all-to-all(f32[4,128,1024]{2,1,0:T(8,128)S(1)} %fusion.46), channel_id=1, replica_groups=mesh['sec'=4,'ch'=64] {'sec'}, dimensions={0} | all-to-all | bytes 4194304 | tf_op jit(solution)/shard_map/all_to_all | solution.py:115
  86.1 6.7 %fusion.42 = f32[1,512,2,512]{3,1,2,0:T(8,128)S(1)} fusion(f32[512,1024,1]{1,0,2:T(8,128)S(1)} %bitcast.191, f32[1024,1,512]{0,2,1:T(8,128)S(1)} %get-tuple-element.22, f32[1024,1,512]{0,2,1:T(8,128)S(1)} %copy-done.2), kind=kOutput, calls=%fused_computation.57 | convolution fusion | flops 6443499520 | bytes 8388608 | tf_op jit(solution)/shard_map/eqy,ynm->emnq/dot_general | solution.py:116
  92.9 3.0 copy.99
  95.8 14.1 %all-to-all-start.1 = ((f32[1,512,2,512]{3,2,0,1:T(2,128)}), f32[1,512,2,512]{3,2,0,1:T(2,128)S(1)}, u32[]{:S(2)}, u32[]{:S(2)}) async-start(f32[1,512,2,512]{3,2,0,1:T(2,128)} %copy.99), calls=%async_computation.1 | async-start | bytes 4194304 | tf_op jit(solution)/shard_map/all_to_all | solution.py:119
  111.4 0.8 copy.103
  112.1 0.7 copy.104
  112.9 0.5 multiply_sine_fusion.1
  113.4 0.7 copy.105
  114.1 0.5 multiply_cosine_fusion.1
  114.6 0.8 copy.93
  115.9 0.3 multiply_sine_fusion.3
  116.2 0.3 multiply_sine_fusion.2
  116.5 1.2 multiply_sine_fusion
  117.7 1.0 fusion.100
  118.7 0.7 maximum_bitcast_fusion.20
  119.4 1.0 fusion.91
  120.5 1.1 fusion.101
  121.6 1.1 maximum_bitcast_fusion.10
  122.7 1.1 maximum_bitcast_fusion.12
  124.0 37.1 %all-to-all-done.1 = f32[1,512,2,512]{3,2,0,1:T(2,128)S(1)} async-done(((f32[1,512,2,512]{3,2,0,1:T(2,128)}), f32[1,512,2,512]{3,2,0,1:T(2,128)S(1)}, u32[]{:S(2)}, u32[]{:S(2)}) %all-to-all-start.1) | async-done | bytes 2097184 | tf_op jit(solution)/shard_map/all_to_all | solution.py:119
  161.1 2.6 copy.151
  163.7 2.1 reshape.706
  165.8 4.7 %fusion.36 = f32[1,8,2,256,128]{3,4,2,1,0:T(8,128)S(1)} fusion(f32[8,2,64,4,128,1]{4,3,2,1,0,5:T(4,128)S(1)} %bitcast.189, f32[1,256,2,64,4]{1,3,4,2,0:T(8,128)} %get-tuple-element.12, f32[1,256,2,64,4]{1,3,4,2,0:T(8,128)} %get-tuple-element.11), kind=kOutput, calls=%fused_computation.55 | convolution fusion | flops 3221487616 | bytes 5242880 | tf_op jit(solution)/shard_map/okrcs,gfrcsj->gfokj/dot_general | solution.py:132
  170.8 3.4 fusion.14
  174.3 1.8 fusion.51
  176.5 0.7 copy-done.7
  177.4 8.2 %fusion.23 = f32[1,8,2,256,128]{3,4,2,1,0:T(8,128)} fusion(f32[1,8,1,256,128]{4,3,2,1,0:T(8,128)S(1)} %get-tuple-element.6, f32[1,8,1,256,128]{4,3,2,1,0:T(8,128)S(1)} %get-tuple-element.5, f32[1,256,2,256]{3,1,2,0:T(8,128)S(1)} %copy-done.8, f32[1,256,2,256]{3,1,2,0:T(8,128)S(1)} %copy-done.7), kind=kOutput, calls=%fused_computation.35 | convolution fusion | flops 3222536192 | bytes 5242880 | tf_op jit(solution)/shard_map/obrk,gfrkj->gfobj/dot_general | solution.py:155
  185.6 1.9 copy.107
  187.5 28.7 %copy.108 = f32[1,8,2,32768]{1,2,0,3:T(2,128)} copy(f32[1,8,2,32768]{3,0,2,1:T(1,128)S(1)} %bitcast.187) | data formatting | bytes 4194304 | tf_op jit(solution)/shard_map/reshape | solution.py:158
  216.3 55.0 %reshape.736 = f32[64,1,8192]{2,1,0:T(1,128)S(1)} reshape(f32[32768,1,2,8]{3,2,1,0:T(2,128)} %bitcast.182) | data formatting | bytes 4194304
  271.3 57.3 %all_to_all.40 = f32[64,1,8192]{2,1,0:T(1,128)} all-to-all(f32[64,1,8192]{2,1,0:T(1,128)S(1)} %reshape.736), channel_id=1, replica_groups=mesh['sec'=4,'ch'=64] {'ch'}, dimensions={0} | all-to-all | bytes 4194304 | tf_op jit(solution)/shard_map/all_to_all | solution.py:159
  328.5 0.6 broadcast.955
  329.1 7.7 %reduce = f32[64,8192]{1,0:T(8,128)S(1)} reduce(f32[64,1,8192]{2,1,0:T(1,128)} %all_to_all.40, f32[]{:T(128)} %broadcast.955), dimensions={1}, to_apply=%all_to_all.33.reduce_sub_computation | reduce | bytes 4194308 | tf_op jit(solution)/shard_map/all_to_all | solution.py:159
  336.8 53.0 %reshape.737 = f32[32768,1,2,8]{3,2,1,0:T(2,128)} reshape(f32[64,8192]{1,0:T(8,128)S(1)} %reduce) | data formatting | bytes 4194304
  389.8 36.5 %copy.138 = f32[1,8,2,64,512]{4,1,3,2,0:T(8,128)} copy(f32[1,8,2,64,512]{1,2,4,3,0:T(2,128)} %bitcast.183) | data formatting | bytes 4194304 | tf_op jit(solution)/shard_map/all_to_all | solution.py:159
  426.3 10.4 %fusion.39 = f32[1,512,1024]{2,1,0:T(8,128)} fusion(f32[1,512,1024]{2,1,0:T(8,128)S(1)} %copy-done.4, f32[1,512,1024]{2,1,0:T(8,128)} %get-tuple-element.25, f32[1,8,2,64,512]{4,1,3,2,0:T(8,128)} %copy.138), kind=kOutput, calls=%fused_computation.56 | convolution fusion | flops 6444548096 | bytes 8388608 | tf_op jit(solution)/shard_map/gfrc,rft->gct/dot_general | solution.py:160
  (59 shorter events, 2.1 us)
Async XLA Ops:
  0.0 21.5 %copy-start = (bf16[64]{0:T(256)(128)(2,1)S(1)}, bf16[64]{0:T(256)(128)(2,1)}, u32[]{:S(2)}) copy-start(bf16[64]{0:T(256)(128)(2,1)} %param.9) | copy-start | bytes 388
  9.2 9.6 %slice-start = ((bf16[4,128,4156]{1,0,2:T(4,128)(2,1)}), bf16[4,128,4096]{1,0,2:T(4,128)(2,1)S(1)}, s32[]{:S(2)}) async-start(bf16[4,128,4156]{1,0,2:T(4,128)(2,1)} %param.8), calls=%async_computation.3 | async-start | bytes 8388608 | tf_op jit(solution)/shard_map/slice | solution.py:71
  18.8 2.7 slice-start.1
  19.3 2.0 copy-start.6
  25.1 3.1 copy-start.2
  34.9 2.0 copy-start.16
  35.0 2.0 copy-start.17
  35.0 3.0 copy-start.5
  35.3 2.7 copy-start.3
  95.8 65.3 %all-to-all-start.1 = ((f32[1,512,2,512]{3,2,0,1:T(2,128)}), f32[1,512,2,512]{3,2,0,1:T(2,128)S(1)}, u32[]{:S(2)}, u32[]{:S(2)}) async-start(f32[1,512,2,512]{3,2,0,1:T(2,128)} %copy.99), calls=%async_computation.1 | async-start | bytes 4194304 | tf_op jit(solution)/shard_map/all_to_all | solution.py:119
  120.5 3.3 copy-start.12
  120.5 3.3 copy-start.13
  165.8 4.7 %copy-start.14 = (f32[256,128]{0,1:T(8,128)S(1)}, f32[256,128]{0,1:T(8,128)}, u32[]{:S(2)}) copy-start(f32[256,128]{0,1:T(8,128)} %get-tuple-element.26) | copy-start | bytes 393220
  165.8 4.7 %copy-start.15 = (f32[256,128]{0,1:T(8,128)S(1)}, f32[256,128]{0,1:T(8,128)}, u32[]{:S(2)}) copy-start(f32[256,128]{0,1:T(8,128)} %get-tuple-element.27) | copy-start | bytes 393220
  170.8 3.5 copy-start.9
  174.3 1.9 copy-start.10
  174.3 1.9 copy-start.11
  176.2 1.0 copy-start.7
  176.2 1.2 copy-start.8
  389.8 36.5 %copy-start.4 = (f32[1,512,1024]{2,1,0:T(8,128)S(1)}, f32[1,512,1024]{2,1,0:T(8,128)}, u32[]{:S(2)}) copy-start(f32[1,512,1024]{2,1,0:T(8,128)} %get-tuple-element.24) | copy-start | bytes 6291460
  426.3 10.4 %copy-start.1 = (bf16[64]{0:T(256)(128)(2,1)S(1)}, bf16[64]{0:T(256)(128)(2,1)}, u32[]{:S(2)}) copy-start(bf16[64]{0:T(256)(128)(2,1)} %param.9) | copy-start | bytes 388
where the time goes:
time: 441 us; the launch traced here: 437 us
  local copies, waits for them, and re-layouts  190 us (43%)
  blocking collectives  87.2 us (20%)
  matrix products  66.8 us (15%)
  other arithmetic  38.1 us (9%)
  waiting for transfers between devices  37.1 us (8%)
  starting transfers between devices  14.1 us (3%)
    unnamed x40, local copies, waits for them, and re-layouts  112 us
    all_to_all x1, blocking collectives, per_device(): lax.all_to_all(passed, 'ch', split_axis=3, concat_axis=1, tiled=True)  57.3 us
    all_to_all x1, waiting for transfers between devices, per_device(): lax.all_to_all(repeated_pass, 'ch', split_axis=1, concat_axis=3, tiled=True)  37.1 us
    all_to_all x2, local copies, waits for them, and re-layouts, per_device(): lax.all_to_all(passed, 'ch', split_axis=3, concat_axis=1, tiled=True)  37.1 us
    all_to_all x1, blocking collectives, per_device(): lax.all_to_all(traces, 'sec', split_axis=0, concat_axis=1, tiled=True)  29.9 us
    reshape x1, local copies, waits for them, and re-layouts, per_device(): passed = passed.reshape(groups, local_bins, 2, total_channels)  28.7 us
    dot_general x1, matrix products, per_device(): jnp.einsum('wfrc,rft->wct', whitened, backward, precision=TOP_FREQUENCY)  18.2 us
    all_to_all x1, starting transfers between devices, per_device(): lax.all_to_all(repeated_pass, 'ch', split_axis=1, concat_axis=3, tiled=True)  14.1 us
  transfers between devices with their start and end apart: 1, of which 1 were waited for; matrix products, arithmetic and copies ran while one was open for 3% of the time, Pallas kernels for 0%

commit v1 on v0

v1 whole, which is shorter than its diff:
```python
import functools
import math

import jax
import jax.numpy as jnp
import ml_dtypes
import numpy as np
from jax import lax
from jax.experimental import pallas as pl
from jax.experimental.pallas import tpu as pltpu
from jax.sharding import PartitionSpec as P

TAPS = 64
DECIM = 4
SMOOTH = 4
FLOOR = 0.05
SAMPLES = 1024
BINS = 512
PAD = 16
ALIGN = 16
OUT = 128
SPAN = DECIM * OUT
INNER = 128
OUTER = 256
SECTIONS = 4
SHARDS = 64
TABLE_ROWS = PAD + BINS + PAD
VARIANTS = (8,)
VMEM_LIMIT = 48 * 1024 * 1024
MESH = pl.DeviceIdType.MESH
VM = pltpu.VMEM
SM = pltpu.SMEM


def split_np(table):
    table = table.astype(np.float32)
    high = table.astype(ml_dtypes.bfloat16)
    low = (table - high.astype(np.float32)).astype(ml_dtypes.bfloat16)
    return high, low


def split(value):
    high = value.astype(jnp.bfloat16)
    low = (value - high.astype(jnp.float32)).astype(jnp.bfloat16)
    return high, low


def mm(a, b):
    return jnp.dot(a, b, preferred_element_type=jnp.float32)


def mm_nt(a, b):
    return lax.dot_general(a, b, (((1,), (1,)), ((), ())), preferred_element_type=jnp.float32)


def time_tables():
    f = np.arange(BINS)[:, None]
    t = np.arange(SAMPLES)[None, :]
    angle = (f * t % SAMPLES) * (2.0 * math.pi / SAMPLES)
    table = np.zeros((2, TABLE_ROWS, SAMPLES))
    table[0, PAD : PAD + BINS] = np.cos(angle) / 32.0
    table[1, PAD : PAD + BINS] = -np.sin(angle) / 32.0
    return split_np(table)


def wave_tables():
    k = np.arange(OUTER)
    angle = (k[:, None] * k[None, :] % OUTER) * (2.0 * math.pi / OUTER)
    c, s = np.cos(angle), np.sin(angle)
    outer = split_np(np.block([[c, s], [-s, c]]))
    outer_back = split_np(np.block([[c, -s], [s, c]]) / (OUTER * INNER))
    j = np.arange(INNER)
    angle = (j[:, None] * j[None, :] % INNER) * (2.0 * math.pi / INNER)
    c, s = np.cos(angle), np.sin(angle)
    inner = split_np(np.block([[c, -s], [s, c]]))
    inner_back = split_np(np.block([[c, s], [-s, c]]))
    angle = k[:, None] * j[None, :] * (2.0 * math.pi / (OUTER * INNER))
    twist = np.stack([np.cos(angle), np.sin(angle)]).astype(np.float32)
    return outer, outer_back, inner, inner_back, twist


def first_bin(scal, nb):
    return jnp.minimum(scal[0], BINS - nb * SHARDS)


def front_kernel(
    nb, scal, strain, taps, weight, table_h, table_l, s_ref, dec, amp, parts
):
    rows = nb * SHARDS
    wide = rows + 2 * PAD
    f0 = pl.multiple_of(first_bin(scal, nb), ALIGN)
    fir = jnp.broadcast_to(taps[...], (OUT, taps.shape[1]))
    fir = pltpu.roll(fir, 0, 1, stride=DECIM, stride_axis=0).astype(jnp.bfloat16)
    tail = SPAN + TAPS - DECIM
    index = f0 + lax.broadcasted_iota(jnp.int32, (rows, INNER), 0)
    band = ((index >= scal[1]) & (index <= scal[2])).astype(jnp.float32)
    scale = band * weight[...]

    def pair(p, carry):
        for w in range(2):
            for q in range(SAMPLES // OUT):
                size = SPAN + OUT if (q + 1) * SPAN + OUT <= strain.shape[2] else tail
                piece = strain[2 * p + w, :, q * SPAN : q * SPAN + size]
                dec[w * INNER : (w + 1) * INNER, q * OUT : (q + 1) * OUT] = mm_nt(
                    piece, fir[:, :size]
                )
        high, low = split(dec[...])
        for part in range(2):
            th = table_h[part, pl.ds(f0, wide), :]
            tl = table_l[part, pl.ds(f0, wide), :]
            parts[part] = mm_nt(th, high) + mm_nt(th, low) + mm_nt(tl, high)
        real, imag = parts[0], parts[1]
        amp[...] = jnp.sqrt(real * real + imag * imag)
        total = amp[PAD - SMOOTH : PAD - SMOOTH + rows, :]
        for d in range(1, 2 * SMOOTH + 1):
            total = total + amp[PAD - SMOOTH + d : PAD - SMOOTH + d + rows, :]
        smooth = total / (2 * SMOOTH + 1)
        smooth = jnp.maximum(smooth, FLOOR)
        for w in range(2):
            lanes = slice(w * INNER, (w + 1) * INNER)
            factor = scale / smooth[:, lanes]
            start = pl.multiple_of((2 * p + w) * SHARDS, SHARDS)
            for part in range(2):
                value = parts[part, PAD : PAD + rows, lanes] * factor
                s_ref[part, :, pl.ds(start, SHARDS), :] = value.reshape(nb, SHARDS, INNER)
        return carry

    lax.fori_loop(0, SECTIONS // 2, pair, 0)


def wave_kernel(
    nb, chunks, scal, s_ref, outer_h, outer_l, back_h, back_l, in_h, in_l, inb_h, inb_l,
    twist, r_ref, x_ref, z_ref, fsend, frecv, bsend, brecv,
):
    sec = lax.axis_index("sec")
    ch = lax.axis_index("ch")
    y, z, core = ch // 16, (ch // 2) % 8, ch % 2
    me = sec * SHARDS + ch

    def each(action, with_sections):
        first = 16 if with_sections else 4

        def run(dz, dc, start):
            def step(q, carry):
                dx, dy = q // 4, q % 4
                to_ch = ((y + dy) % 4) * 16 + ((z + dz) % 8) * 2 + (core + dc) % 2
                action((sec + dx) % 4, to_ch)
                return carry

            lax.fori_loop(start, first, step, 0)

        for dz in (4, 3, 5, 2, 6, 1, 7):
            for dc in range(2):
                run(dz, dc, 0)
        run(0, 1, 0)
        run(0, 0, 1)

    barrier = pltpu.get_barrier_semaphore()
    each(
        lambda w, b: pl.semaphore_signal(
            barrier, inc=1, device_id=(w, b), device_id_type=MESH
        ),
        True,
    )
    pl.semaphore_wait(barrier, SECTIONS * SHARDS - 1)

    for n, (lo, size) in enumerate(chunks):
        bins = pl.ds(lo, size)
        pltpu.make_async_copy(
            s_ref.at[:, bins, pl.ds(me, 1)], x_ref.at[:, bins, pl.ds(me, 1)], frecv.at[n]
        ).start()

        def forward(w, b):
            pltpu.make_async_remote_copy(
                src_ref=s_ref.at[:, bins, pl.ds(w * SHARDS + b, 1)],
                dst_ref=x_ref.at[:, bins, pl.ds(me, 1)],
                send_sem=fsend.at[n],
                recv_sem=frecv.at[n],
                device_id=(w, b),
                device_id_type=MESH,
            ).start()

        each(forward, True)

    k1 = lax.broadcasted_iota(jnp.int32, (OUTER, INNER), 0)
    k2 = lax.broadcasted_iota(jnp.int32, (OUTER, INNER), 1)
    k = k1 + OUTER * k2
    spacing = jnp.minimum(k, OUTER * INNER - k)
    slow = scal[3] * spacing
    fast = scal[4] * spacing
    rate = 500 * OUTER * INNER // SAMPLES
    cosine, sine = twist[0], twist[1]

    def transform(jj, count):
        lanes = [slice(i * INNER, (i + 1) * INNER) for i in range(count)]
        field = jnp.concatenate(
            [
                jnp.concatenate([x_ref[part, jj + i] for i in range(count)], axis=1)
                for part in range(2)
            ],
            axis=0,
        )
        high, low = split(field)
        field = mm(outer_h[...], high) + mm(outer_h[...], low) + mm(outer_l[...], high)
        stacked = []
        for i in range(count):
            real, imag = field[:OUTER, lanes[i]], field[OUTER:, lanes[i]]
            stacked.append(
                jnp.concatenate(
                    [real * cosine + imag * sine, imag * cosine - real * sine], axis=1
                )
            )
        high, low = split(jnp.concatenate(stacked, axis=0))
        field = mm(high, in_h[...]) + mm(low, in_h[...]) + mm(high, in_l[...])
        masked = []
        for i in range(count):
            reach = (first_bin(scal, nb) + (jj + i) * SHARDS + ch) * rate
            fan = ((slow <= reach) & (reach <= fast)).astype(jnp.float32)
            block = field[i * OUTER : (i + 1) * OUTER]
            masked.append(
                jnp.concatenate([block[:, :INNER] * fan, block[:, INNER:] * fan], axis=1)
            )
        high, low = split(jnp.concatenate(masked, axis=0))
        field = mm(high, inb_h[...]) + mm(low, inb_h[...]) + mm(high, inb_l[...])
        reals, imags = [], []
        for i in range(count):
            block = field[i * OUTER : (i + 1) * OUTER]
            real, imag = block[:, :INNER], block[:, INNER:]
            reals.append(real * cosine - imag * sine)
            imags.append(imag * cosine + real * sine)
        field = jnp.concatenate(
            [jnp.concatenate(reals, axis=1), jnp.concatenate(imags, axis=1)], axis=0
        )
        high, low = split(field)
        field = mm(back_h[...], high) + mm(back_h[...], low) + mm(back_l[...], high)
        for i in range(count):
            z_ref[0, jj + i] = field[:OUTER, lanes[i]]
            z_ref[1, jj + i] = field[OUTER:, lanes[i]]

    for n, (lo, size) in enumerate(chunks):
        bins = pl.ds(lo, size)
        whole = x_ref.at[:, bins]
        pltpu.make_async_copy(whole, whole, frecv.at[n]).wait()
        if size // 2:

            def two(i, carry):
                transform(lo + 2 * i, 2)
                return carry

            lax.fori_loop(0, size // 2, two, 0)
        if size % 2:
            transform(lo + size - 1, 1)
        pltpu.make_async_copy(
            z_ref.at[:, bins, pl.ds(4 * ch, 4)], r_ref.at[:, bins, pl.ds(4 * ch, 4)], brecv.at[n]
        ).start()

        def backward(w, c):
            pltpu.make_async_remote_copy(
                src_ref=z_ref.at[:, bins, pl.ds(4 * c, 4)],
                dst_ref=r_ref.at[:, bins, pl.ds(4 * ch, 4)],
                send_sem=bsend.at[n],
                recv_sem=brecv.at[n],
                device_id=(sec, c),
                device_id_type=MESH,
            ).start()

        each(backward, False)

    for n, (lo, size) in enumerate(chunks):
        bins = pl.ds(lo, size)
        whole = r_ref.at[:, bins]
        pltpu.make_async_copy(whole, whole, brecv.at[n]).wait()
        sent = z_ref.at[:, bins, pl.ds(0, OUTER - 4)]
        pltpu.make_async_copy(sent, sent, bsend.at[n]).wait()
        sent = s_ref.at[:, bins, pl.ds(0, OUTER - 1)]
        pltpu.make_async_copy(sent, sent, fsend.at[n]).wait()


def final_kernel(nb, scal, r_ref, table_h, table_l, out_ref, turned_h, turned_l):
    rows = nb * SHARDS
    f0 = pl.multiple_of(first_bin(scal, nb), ALIGN)
    for block in range(4):
        for part in range(2):
            value = r_ref[part, pl.ds(block, rows, stride=4), :] * 2.0
            high, low = split(value.T)
            turned_h[part, block * INNER : (block + 1) * INNER, :] = high
            turned_l[part, block * INNER : (block + 1) * INNER, :] = low

    def column(n, carry):
        cols = pl.ds(pl.multiple_of(n * 256, 256), 256)
        total = jnp.zeros((4 * INNER, 256), jnp.float32)
        for part in range(2):
            th = table_h[part, pl.ds(f0 + PAD, rows), cols]
            tl = table_l[part, pl.ds(f0 + PAD, rows), cols]
            total = total + mm(turned_h[part], th)
            total = total + mm(turned_l[part], th)
            total = total + mm(turned_h[part], tl)
        out_ref[:, cols] = total
        return carry

    lax.fori_loop(0, SAMPLES // 256, column, 0)


def chunks_of(nb):
    first = (nb + 1) // 2
    first += first % 2 if nb > 2 else 0
    return [(0, first), (first, nb - first)] if nb > first else [(0, nb)]


def branch(nb, scal, strain, taps, weight, table_h, table_l, *waves):
    rows = nb * SHARDS
    wide = rows + 2 * PAD
    smem = pl.BlockSpec(memory_space=SM)
    vmem = pl.BlockSpec(memory_space=VM)
    spectrum = pl.pallas_call(
        functools.partial(front_kernel, nb),
        out_shape=jax.ShapeDtypeStruct((2, nb, SECTIONS * SHARDS, INNER), jnp.float32),
        in_specs=[smem] + [vmem] * 5,
        out_specs=vmem,
        scratch_shapes=[
            VM((2 * INNER, SAMPLES), jnp.float32),
            VM((wide, 2 * INNER), jnp.float32),
            VM((2, wide, 2 * INNER), jnp.float32),
        ],
        compiler_params=pltpu.CompilerParams(vmem_limit_bytes=VMEM_LIMIT),
        name=f"front{nb}",
    )(scal, strain, taps, weight, table_h, table_l)
    chunks = chunks_of(nb)
    count = len(chunks)
    dma = pltpu.SemaphoreType.DMA((count,))
    field = jax.ShapeDtypeStruct((2, nb, OUTER, INNER), jnp.float32)
    passed = pl.pallas_call(
        functools.partial(wave_kernel, nb, chunks),
        out_shape=field,
        in_specs=[smem] + [vmem] * 10,
        out_specs=vmem,
        scratch_shapes=[VM(field.shape, jnp.float32), VM(field.shape, jnp.float32)] + [dma] * 4,
        compiler_params=pltpu.CompilerParams(
            vmem_limit_bytes=VMEM_LIMIT, has_side_effects=True, collective_id=nb
        ),
        name=f"wave{nb}",
    )(scal, spectrum, *waves)
    passed = passed.reshape(2, nb * OUTER, INNER)
    return pl.pallas_call(
        functools.partial(final_kernel, nb),
        out_shape=jax.ShapeDtypeStruct((4 * INNER, SAMPLES), jnp.float32),
        in_specs=[smem] + [vmem] * 3,
        out_specs=vmem,
        scratch_shapes=[VM((2, 4 * INNER, rows), jnp.bfloat16)] * 2,
        compiler_params=pltpu.CompilerParams(vmem_limit_bytes=VMEM_LIMIT),
        name=f"final{nb}",
    )(scal, passed, table_h, table_l)


def per_device(
    strain_rate, fir_taps, gain_code, alive_mask, band_low, band_high, slow_limit, fast_limit
):
    table_h, table_l = time_tables()
    outer, outer_back, inner, inner_back, twist = wave_tables()
    f0 = band_low // ALIGN * ALIGN
    scal = jnp.concatenate([f0, band_low, band_high, slow_limit, fast_limit])
    taps = jnp.pad(fir_taps.astype(jnp.float32)[None, :], ((0, 0), (0, SPAN + OUT - TAPS)))
    weight = (gain_code.astype(jnp.float32) * 0.25 * alive_mask.astype(jnp.float32))[None, :]
    args = (scal, strain_rate, taps, weight, table_h, table_l)
    args = args + outer + outer_back + inner + inner_back + (twist,)
    args = tuple(jnp.asarray(a) for a in args)
    if len(VARIANTS) == 1:
        out = branch(VARIANTS[0], *args)
    else:
        need = (band_high - f0)[0] // SHARDS + 1
        which = sum((need > nb).astype(jnp.int32) for nb in VARIANTS[:-1])
        out = lax.switch(which, [functools.partial(branch, nb) for nb in VARIANTS], *args)
    return out[None]


def solution(mesh):
    placed = (
        P(None, ("sec", "ch"), None),
        P(),
        P(("sec", "ch")),
        P(("sec", "ch")),
        P(),
        P(),
        P(),
        P(),
    )
    return jax.shard_map(
        per_device, mesh=mesh, in_specs=placed, out_specs=P("sec", "ch", None), check_vma=False
    )
```

time: 441 us -> 144 us (0.33)
  local copies, waits for them, and re-layouts: 190 us -> 9.52 us
  Pallas kernels: 0 us -> 130 us
  blocking collectives: 87.2 us -> 0 us
  matrix products: 66.8 us -> 0 us
  waiting for transfers between devices: 37.1 us -> 0 us
  other arithmetic: 38.1 us -> 1.34 us
  starting transfers between devices: 14.1 us -> 0 us
    pallas_call x0 -> x3, Pallas kernels: none -> 130 us  [the longest x1 112 us: branch(): pl.pallas_call(functools.partial(wave_kernel, nb, chunks), out_shape=fiel...]
    unnamed x40 -> x23, local copies, waits for them, and re-layouts: 112 us -> 9.44 us
    all_to_all x2 -> x0, blocking collectives: 87.2 us -> none  [the longest x1 57.3 us: per_device(): lax.all_to_all(passed, 'ch', split_axis=3, concat_axis=1, tiled=True)]
    dot_general x12 -> x0, matrix products: 66.8 us -> none  [the longest x1 18.2 us: per_device(): jnp.einsum('wfrc,rft->wct', whitened, backward, precision=TOP_FREQUENCY)]
    all_to_all x3 -> x0, local copies, waits for them, and re-layouts: 39.6 us -> none  [the longest x2 37.1 us: per_device(): lax.all_to_all(passed, 'ch', split_axis=3, concat_axis=1, tiled=True)]
    all_to_all x1 -> x0, waiting for transfers between devices: 37.1 us -> none  [per_device(): lax.all_to_all(repeated_pass, 'ch', split_axis=1, concat_axis=3, tiled=True)]
    reshape x1 -> x0, local copies, waits for them, and re-layouts: 28.7 us -> none  [per_device(): passed = passed.reshape(groups, local_bins, 2, total_channels)]
    all_to_all x1 -> x0, starting transfers between devices: 14.1 us -> none  [per_device(): lax.all_to_all(repeated_pass, 'ch', split_axis=1, concat_axis=3, tiled=True)]
  transfers between devices with their start and end apart: 1 -> 0, of which waited for: 1 -> 0; matrix products, arithmetic and copies ran while one was open for 3% -> 0% of each run, Pallas kernels for 0% -> 0%
where the time goes in v1:
time: 144 us
  Pallas kernels  130 us (90%)
  local copies, waits for them, and re-layouts  9.52 us (7%)
  between operations  2.74 us (2%)
    pallas_call x1, Pallas kernels, branch(): pl.pallas_call(functools.partial(wave_kernel, nb, chunks), out_shape=fiel...  112 us
    pallas_call x1, Pallas kernels, branch(): pl.pallas_call(functools.partial(front_kernel, nb), out_shape=jax.ShapeDt...  10.2 us
    unnamed x23, local copies, waits for them, and re-layouts  9.44 us
    pallas_call x1, Pallas kernels, branch(): pl.pallas_call(functools.partial(final_kernel, nb), out_shape=jax.ShapeDt...  7.56 us

profile of v1, /device:TPU:1, one launch (start us, length us, event | category | flops | bytes accessed | tf_op | source)
XLA Modules:
  0.0 143.7 jit_solution(2463097370760602822)
XLA Ops:
  2.6 0.1 concatenate.3.scal
  2.7 0.7 multiply_bitcast_fusion.weight
  3.4 0.7 pad_convert_fusion.taps
  4.0 0.0 copy-start
  4.0 8.1 %copy.20.strain = bf16[4,128,4156]{2,1,0:T(8,128)(2,1)} copy(bf16[4,128,4156]{1,0,2:T(4,128)(2,1)} %param.19) | data formatting | bytes 8511488 | tf_op args[0]
  12.1 0.0 copy-done
  12.1 0.0 copy-start.2
  12.1 0.0 copy-start.3
  12.1 0.0 copy-start.4
  12.1 0.0 copy-start.5
  12.1 0.0 copy-start.6
  12.1 0.0 copy-start.7
  12.2 0.0 copy-start.8
  12.2 0.0 copy-start.9
  12.2 0.0 copy-start.10
  12.2 10.2 %front8.1.s_ref = f32[2,8,256,128]{3,2,1,0:T(8,128)S(1)} custom-call(s32[5]{0:T(128)S(1)} %concatenate.3.scal, bf16[4,128,4156]{2,1,0:T(8,128)(2,1)} %copy.20.strain, f32[1,640]{1,0:T(1,128)S(1)} %pad_convert_fusion.taps, f32[1,128]{1,0:T(1,128)S(1)} %multiply_bitcast_fusion.weight, bf16[2,544,1024]{2,1,0:T(8,128)(2,1)S(1)} %copy-done, ...), custom_call_target="tpu_custom_call" | custom-call | tf_op jit(solution)/shard_map/front8/pallas_call | solution.py:315
  22.4 0.0 copy-start.1
  22.4 1.3 copy-done.1
  23.8 0.0 copy-done.2
  23.8 0.0 copy-done.3
  23.8 0.0 copy-done.4
  23.8 0.0 copy-done.5
  23.8 0.0 copy-done.6
  23.8 0.0 copy-done.7
  23.8 0.0 copy-done.8
  23.8 0.0 copy-done.9
  23.8 0.0 copy-done.10
  23.8 112.3 %wave8.1 = f32[2,8,256,128]{3,2,1,0:T(8,128)S(1)} custom-call(s32[5]{0:T(128)S(1)} %concatenate.3.scal, f32[2,8,256,128]{3,2,1,0:T(8,128)} %copy-done.1, bf16[512,512]{1,0:T(8,128)(2,1)S(1)} %copy-done.5, bf16[512,512]{1,0:T(8,128)(2,1)S(1)} %copy-done.4, bf16[512,512]{1,0:T(8,128)(2,1)S(1)} %copy-done.3, bf16[512,512]{1,0:T(8,128)(2,1)S(1)} %copy-done.2, ...), custom_call_target="tpu_custom_call" | custom-call | tf_op jit(solution)/shard_map/wave8/pallas_call | solution.py:332
  136.2 7.6 %final8.1 = f32[512,1024]{1,0:T(8,128)} custom-call(s32[5]{0:T(128)S(1)} %concatenate.3.scal, f32[2,2048,128]{2,1,0:T(8,128)S(1)} %bitcast.5, bf16[2,544,1024]{2,1,0:T(8,128)(2,1)S(1)} %copy-done, bf16[2,544,1024]{2,1,0:T(8,128)(2,1)} %constant.53.clone.table_l), custom_call_target="tpu_custom_call" | custom-call | tf_op jit(solution)/shard_map/final8/pallas_call | solution.py:344
Async XLA Ops:
  4.0 8.1 %copy-start = (bf16[2,544,1024]{2,1,0:T(8,128)(2,1)S(1)}, bf16[2,544,1024]{2,1,0:T(8,128)(2,1)}, u32[]{:S(2)}) copy-start(bf16[2,544,1024]{2,1,0:T(8,128)(2,1)} %constant.52.clone.table_h) | copy-start | bytes 6684676
  12.1 11.7 %copy-start.2 = (bf16[512,512]{1,0:T(8,128)(2,1)S(1)}, bf16[512,512]{1,0:T(8,128)(2,1)}, u32[]{:S(2)}) copy-start(bf16[512,512]{1,0:T(8,128)(2,1)} %constant.57.clone.back_l) | copy-start | bytes 1572868
  12.1 11.7 %copy-start.3 = (bf16[512,512]{1,0:T(8,128)(2,1)S(1)}, bf16[512,512]{1,0:T(8,128)(2,1)}, u32[]{:S(2)}) copy-start(bf16[512,512]{1,0:T(8,128)(2,1)} %constant.56.clone.back_h) | copy-start | bytes 1572868
  12.1 11.7 %copy-start.4 = (bf16[512,512]{1,0:T(8,128)(2,1)S(1)}, bf16[512,512]{1,0:T(8,128)(2,1)}, u32[]{:S(2)}) copy-start(bf16[512,512]{1,0:T(8,128)(2,1)} %constant.55.clone.outer_l) | copy-start | bytes 1572868
  12.1 11.7 %copy-start.5 = (bf16[512,512]{1,0:T(8,128)(2,1)S(1)}, bf16[512,512]{1,0:T(8,128)(2,1)}, u32[]{:S(2)}) copy-start(bf16[512,512]{1,0:T(8,128)(2,1)} %constant.54.clone.outer_h) | copy-start | bytes 1572868
  12.1 11.6 %copy-start.6 = (f32[2,256,128]{2,1,0:T(8,128)S(1)}, f32[2,256,128]{2,1,0:T(8,128)}, u32[]{:S(2)}) copy-start(f32[2,256,128]{2,1,0:T(8,128)} %constant.62.clone.twist) | copy-start | bytes 786436
  12.1 11.6 %copy-start.7 = (bf16[256,256]{1,0:T(8,128)(2,1)S(1)}, bf16[256,256]{1,0:T(8,128)(2,1)}, u32[]{:S(2)}) copy-start(bf16[256,256]{1,0:T(8,128)(2,1)} %constant.61.clone.inb_l) | copy-start | bytes 393220
  12.2 11.6 %copy-start.8 = (bf16[256,256]{1,0:T(8,128)(2,1)S(1)}, bf16[256,256]{1,0:T(8,128)(2,1)}, u32[]{:S(2)}) copy-start(bf16[256,256]{1,0:T(8,128)(2,1)} %constant.60.clone.inb_h) | copy-start | bytes 393220
  12.2 11.6 %copy-start.9 = (bf16[256,256]{1,0:T(8,128)(2,1)S(1)}, bf16[256,256]{1,0:T(8,128)(2,1)}, u32[]{:S(2)}) copy-start(bf16[256,256]{1,0:T(8,128)(2,1)} %constant.59.clone.in_l) | copy-start | bytes 393220
  12.2 11.6 %copy-start.10 = (bf16[256,256]{1,0:T(8,128)(2,1)S(1)}, bf16[256,256]{1,0:T(8,128)(2,1)}, u32[]{:S(2)}) copy-start(bf16[256,256]{1,0:T(8,128)(2,1)} %constant.58.clone.in_h) | copy-start | bytes 393220
  22.4 1.3 copy-start.1

commit v2 on v1

--- a/solution.py
+++ b/solution.py
@@ -18,14 +18,14 @@
 BINS = 512
 PAD = 16
 ALIGN = 16
-OUT = 128
-SPAN = DECIM * OUT
+FIR_OUT = TAPS // DECIM
+FIR_ROWS = 256
 INNER = 128
 OUTER = 256
 SECTIONS = 4
 SHARDS = 64
 TABLE_ROWS = PAD + BINS + PAD
-VARIANTS = (8,)
+VARIANTS = (2, 4, 6, 8)
 VMEM_LIMIT = 48 * 1024 * 1024
 MESH = pl.DeviceIdType.MESH
 VM = pltpu.VMEM
@@ -47,10 +47,6 @@
 
 def mm(a, b):
     return jnp.dot(a, b, preferred_element_type=jnp.float32)
-
-
-def mm_nt(a, b):
-    return lax.dot_general(a, b, (((1,), (1,)), ((), ())), preferred_element_type=jnp.float32)
 
 
 def time_tables():
@@ -83,32 +79,61 @@
     return jnp.minimum(scal[0], BINS - nb * SHARDS)
 
 
+def fir_matrix(taps, sections):
+    outputs = 2 * FIR_OUT
+    width = 2 * FIR_ROWS
+    base = jnp.broadcast_to(taps, (outputs, width))
+    base = pltpu.roll(base, FIR_ROWS, 1, stride=DECIM * sections, stride_axis=0)[:, :FIR_ROWS]
+    column = lax.broadcasted_iota(jnp.int32, (outputs, FIR_ROWS), 1)
+    rows = [jnp.where(column % sections == w, base, 0.0) for w in range(sections)]
+    return jnp.concatenate(rows, axis=0).astype(jnp.bfloat16)
+
+
+def decimate(strain, taps, dec):
+    matrix = fir_matrix(taps[...], SECTIONS)
+    blocks = SAMPLES // FIR_OUT
+    outputs = 2 * FIR_OUT
+
+    def add(product, lanes, block, upper):
+        for w in range(SECTIONS):
+            top = w * outputs + (FIR_OUT if upper else 0)
+            where = slice(block * FIR_OUT, (block + 1) * FIR_OUT)
+            value = product[top : top + FIR_OUT, lanes]
+            if upper:
+                dec[w, where, :] = value
+            else:
+                dec[w, where, :] += value
+
+    for first in range(0, blocks, 2):
+        pieces = [strain[n * FIR_ROWS : (n + 1) * FIR_ROWS, :] for n in (first, first + 1)]
+        product = mm(matrix, jnp.concatenate(pieces, axis=1))
+        for n in (first, first + 1):
+            lanes = slice((n - first) * INNER, (n - first + 1) * INNER)
+            add(product, lanes, n, True)
+            if n:
+                add(product, lanes, n - 1, False)
+    last = strain.shape[0] - blocks * FIR_ROWS
+    product = mm(matrix[:, :last], strain[blocks * FIR_ROWS :, :])
+    add(product, slice(0, INNER), blocks - 1, False)
+
+
 def front_kernel(
     nb, scal, strain, taps, weight, table_h, table_l, s_ref, dec, amp, parts
 ):
     rows = nb * SHARDS
     wide = rows + 2 * PAD
     f0 = pl.multiple_of(first_bin(scal, nb), ALIGN)
-    fir = jnp.broadcast_to(taps[...], (OUT, taps.shape[1]))
-    fir = pltpu.roll(fir, 0, 1, stride=DECIM, stride_axis=0).astype(jnp.bfloat16)
-    tail = SPAN + TAPS - DECIM
     index = f0 + lax.broadcasted_iota(jnp.int32, (rows, INNER), 0)
     band = ((index >= scal[1]) & (index <= scal[2])).astype(jnp.float32)
     scale = band * weight[...]
+    decimate(strain, taps, dec)
 
     def pair(p, carry):
-        for w in range(2):
-            for q in range(SAMPLES // OUT):
-                size = SPAN + OUT if (q + 1) * SPAN + OUT <= strain.shape[2] else tail
-                piece = strain[2 * p + w, :, q * SPAN : q * SPAN + size]
-                dec[w * INNER : (w + 1) * INNER, q * OUT : (q + 1) * OUT] = mm_nt(
-                    piece, fir[:, :size]
-                )
-        high, low = split(dec[...])
+        high, low = split(jnp.concatenate([dec[2 * p], dec[2 * p + 1]], axis=1))
         for part in range(2):
             th = table_h[part, pl.ds(f0, wide), :]
             tl = table_l[part, pl.ds(f0, wide), :]
-            parts[part] = mm_nt(th, high) + mm_nt(th, low) + mm_nt(tl, high)
+            parts[part] = mm(th, high) + mm(th, low) + mm(tl, high)
         real, imag = parts[0], parts[1]
         amp[...] = jnp.sqrt(real * real + imag * imag)
         total = amp[PAD - SMOOTH : PAD - SMOOTH + rows, :]
@@ -318,7 +343,7 @@
         in_specs=[smem] + [vmem] * 5,
         out_specs=vmem,
         scratch_shapes=[
-            VM((2 * INNER, SAMPLES), jnp.float32),
+            VM((SECTIONS, SAMPLES, INNER), jnp.float32),
             VM((wide, 2 * INNER), jnp.float32),
             VM((2, wide, 2 * INNER), jnp.float32),
         ],
@@ -359,9 +384,11 @@
     outer, outer_back, inner, inner_back, twist = wave_tables()
     f0 = band_low // ALIGN * ALIGN
     scal = jnp.concatenate([f0, band_low, band_high, slow_limit, fast_limit])
-    taps = jnp.pad(fir_taps.astype(jnp.float32)[None, :], ((0, 0), (0, SPAN + OUT - TAPS)))
+    taps = jnp.repeat(fir_taps.astype(jnp.float32), SECTIONS)[None, :]
+    taps = jnp.pad(taps, ((0, 0), (0, FIR_ROWS)))
+    strain = jnp.transpose(strain_rate, (2, 0, 1)).reshape(-1, INNER)
     weight = (gain_code.astype(jnp.float32) * 0.25 * alive_mask.astype(jnp.float32))[None, :]
-    args = (scal, strain_rate, taps, weight, table_h, table_l)
+    args = (scal, strain, taps, weight, table_h, table_l)
     args = args + outer + outer_back + inner + inner_back + (twist,)
     args = tuple(jnp.asarray(a) for a in args)
     if len(VARIANTS) == 1:

time: 144 us -> 109 us (0.76)
  Pallas kernels: 130 us -> 104 us
  local copies, waits for them, and re-layouts: 9.52 us -> 0.34 us
    pallas_call x1, Pallas kernels: 112 us -> 89 us  [branch(): pl.pallas_call(functools.partial(wave_kernel, nb, chunks), out_shape=fiel...]
    unnamed x23 -> x0, local copies, waits for them, and re-layouts: 9.44 us -> none
    convert_element_type x0 -> x3, other arithmetic: none -> 1.97 us  [the longest x1 0.66 us: per_device(): taps = jnp.repeat(fir_taps.astype(jnp.float32), SECTIONS)[None, :]]
    pallas_call x1, Pallas kernels: 10.2 us -> 8.51 us  [branch(): pl.pallas_call(functools.partial(front_kernel, nb), out_shape=jax.ShapeDt...]
where the time goes in v2:
time: 109 us
  Pallas kernels  104 us (95%)
  between operations  2.64 us (2%)
  other arithmetic  1.98 us (2%)
    pallas_call x1, Pallas kernels, branch(): pl.pallas_call(functools.partial(wave_kernel, nb, chunks), out_shape=fiel...  89 us
    pallas_call x1, Pallas kernels, branch(): pl.pallas_call(functools.partial(front_kernel, nb), out_shape=jax.ShapeDt...  8.51 us
    pallas_call x1, Pallas kernels, branch(): pl.pallas_call(functools.partial(final_kernel, nb), out_shape=jax.ShapeDt...  6.23 us

profile of v2, /device:TPU:1, one launch (start us, length us, event | category | flops | bytes accessed | tf_op | source)
XLA Modules:
  0.0 108.9 jit_solution(5144376540084971284)
XLA Ops:
  2.6 0.1 concatenate.3
  2.7 0.7 convert_element_type.23
  3.4 0.7 convert_element_type.24
  4.0 0.7 convert_element_type.25
  4.7 104.2 %conditional.1 = (f32[1,512,1024]{2,1,0:T(8,128)}) conditional(s32[]{:T(128)} %clamp.3, (bf16[4156,4,128]{2,1,0:T(4,128)(2,1)}, f32[64]{0:T(128)S(1)}, f32[128]{0:T(128)S(1)}, f32[128]{0:T(128)S(1)}, s32[5]{0:T(128)S(1)}, /*index=5*/bf16[2,544,1024]{2,1,0:T(8,128)(2,1)}, bf16[2,544,1024]{2,1,0:T(8,128)(2,1)}, ...), branch_computations={%region_0.1_spmd, %region_1.2_spmd, %region_2.3_spmd, %region_3.4_... | conditional | flops 256 | bytes 29368384 | solution.py:399
  4.7 0.1 broadcast_in_dim.45
  4.8 0.1 broadcast_in_dim_reshape.15
  4.9 0.0 copy-start.10
  4.9 0.0 copy-start.14
  4.9 0.0 copy-start.18
  4.9 0.0 copy-start.22
  4.9 0.0 copy-start.26
  5.0 0.0 copy-start.30
  5.0 0.0 copy-start.34
  5.0 0.0 copy-start.38
  5.0 0.0 copy-start.42
  5.0 8.5 %front6.1.s_ref = f32[2,6,256,128]{3,2,1,0:T(8,128)S(1)} custom-call(s32[5]{0:T(128)S(1)} %get-tuple-element.291.scal, bf16[16624,128]{1,0:T(8,128)(2,1)} %bitcast.32, f32[1,512]{1,0:T(1,128)S(1)} %pad.16.taps, f32[1,128]{1,0:T(1,128)S(1)} %multiply_bitcast_fusion.2.weight, bf16[2,544,1024]{2,1,0:T(8,128)(2,1)} %get-tuple-element.296.table_h, ...), custom_call_target="tpu_custom_call" | custom-call | tf_op jit(solution)/shard_map/cond/branch_2_fun/front6/pallas_call | solution.py:340
  13.5 0.0 copy-done.10
  13.5 0.0 copy-done.14
  13.5 0.0 copy-done.18
  13.6 0.0 copy-done.22
  13.6 0.0 copy-done.26
  13.6 0.0 copy-done.30
  13.6 0.0 copy-done.34
  13.6 0.0 copy-done.38
  13.6 0.0 copy-done.42
  13.6 0.0 copy-start.2
  13.6 0.0 copy-start.6
  13.6 89.0 %wave6.2 = f32[2,6,256,128]{3,2,1,0:T(8,128)S(1)} custom-call(s32[5]{0:T(128)S(1)} %get-tuple-element.291.scal, f32[2,6,256,128]{3,2,1,0:T(8,128)S(1)} %front6.1.s_ref, bf16[512,512]{1,0:T(8,128)(2,1)S(1)} %copy-done.22, bf16[512,512]{1,0:T(8,128)(2,1)S(1)} %copy-done.18, bf16[512,512]{1,0:T(8,128)(2,1)S(1)} %copy-done.14, bf16[512,512]{1,0:T(8,128)(2,1)S(1)} %copy-done.10, ...), custom_call_target="tpu_custom_call" | custom-call | tf_op jit(solution)/shard_map/cond/branch_2_fun/wave6/pallas_call | solution.py:357
  102.6 0.0 copy-done.2
  102.7 0.0 copy-done.6
  102.7 6.2 %final6.2 = f32[512,1024]{1,0:T(8,128)} custom-call(s32[5]{0:T(128)S(1)} %get-tuple-element.291.scal, f32[2,1536,128]{2,1,0:T(8,128)S(1)} %bitcast.23, bf16[2,544,1024]{2,1,0:T(8,128)(2,1)S(1)} %copy-done.6, bf16[2,544,1024]{2,1,0:T(8,128)(2,1)S(1)} %copy-done.2), custom_call_target="tpu_custom_call" | custom-call | tf_op jit(solution)/shard_map/cond/branch_2_fun/final6/pallas_call | solution.py:369
  (2 shorter events, 0.0 us)
Async XLA Ops:
  4.9 8.6 %copy-start.10 = (bf16[512,512]{1,0:T(8,128)(2,1)S(1)}, bf16[512,512]{1,0:T(8,128)(2,1)}, u32[]{:S(2)}) copy-start(bf16[512,512]{1,0:T(8,128)(2,1)} %get-tuple-element.301.back_l) | copy-start | bytes 1572868 | tf_op jit(solution)/shard_map/cond
  4.9 8.6 %copy-start.14 = (bf16[512,512]{1,0:T(8,128)(2,1)S(1)}, bf16[512,512]{1,0:T(8,128)(2,1)}, u32[]{:S(2)}) copy-start(bf16[512,512]{1,0:T(8,128)(2,1)} %get-tuple-element.300.back_h) | copy-start | bytes 1572868 | tf_op jit(solution)/shard_map/cond
  4.9 8.6 %copy-start.18 = (bf16[512,512]{1,0:T(8,128)(2,1)S(1)}, bf16[512,512]{1,0:T(8,128)(2,1)}, u32[]{:S(2)}) copy-start(bf16[512,512]{1,0:T(8,128)(2,1)} %get-tuple-element.299.outer_l) | copy-start | bytes 1572868 | tf_op jit(solution)/shard_map/cond
  4.9 8.6 %copy-start.22 = (bf16[512,512]{1,0:T(8,128)(2,1)S(1)}, bf16[512,512]{1,0:T(8,128)(2,1)}, u32[]{:S(2)}) copy-start(bf16[512,512]{1,0:T(8,128)(2,1)} %get-tuple-element.298.outer_h) | copy-start | bytes 1572868 | tf_op jit(solution)/shard_map/cond
  4.9 8.6 %copy-start.26 = (f32[2,256,128]{2,1,0:T(8,128)S(1)}, f32[2,256,128]{2,1,0:T(8,128)}, u32[]{:S(2)}) copy-start(f32[2,256,128]{2,1,0:T(8,128)} %get-tuple-element.306.twist) | copy-start | bytes 786436 | tf_op jit(solution)/shard_map/cond
  5.0 8.6 %copy-start.30 = (bf16[256,256]{1,0:T(8,128)(2,1)S(1)}, bf16[256,256]{1,0:T(8,128)(2,1)}, u32[]{:S(2)}) copy-start(bf16[256,256]{1,0:T(8,128)(2,1)} %get-tuple-element.305.inb_l) | copy-start | bytes 393220 | tf_op jit(solution)/shard_map/cond
  5.0 8.6 %copy-start.34 = (bf16[256,256]{1,0:T(8,128)(2,1)S(1)}, bf16[256,256]{1,0:T(8,128)(2,1)}, u32[]{:S(2)}) copy-start(bf16[256,256]{1,0:T(8,128)(2,1)} %get-tuple-element.304.inb_h) | copy-start | bytes 393220 | tf_op jit(solution)/shard_map/cond
  5.0 8.6 %copy-start.38 = (bf16[256,256]{1,0:T(8,128)(2,1)S(1)}, bf16[256,256]{1,0:T(8,128)(2,1)}, u32[]{:S(2)}) copy-start(bf16[256,256]{1,0:T(8,128)(2,1)} %get-tuple-element.303.in_l) | copy-start | bytes 393220 | tf_op jit(solution)/shard_map/cond
  5.0 8.6 %copy-start.42 = (bf16[256,256]{1,0:T(8,128)(2,1)S(1)}, bf16[256,256]{1,0:T(8,128)(2,1)}, u32[]{:S(2)}) copy-start(bf16[256,256]{1,0:T(8,128)(2,1)} %get-tuple-element.302.in_h) | copy-start | bytes 393220 | tf_op jit(solution)/shard_map/cond
  13.6 89.0 %copy-start.2 = (bf16[2,544,1024]{2,1,0:T(8,128)(2,1)S(1)}, bf16[2,544,1024]{2,1,0:T(8,128)(2,1)}, u32[]{:S(2)}) copy-start(bf16[2,544,1024]{2,1,0:T(8,128)(2,1)} %get-tuple-element.297.table_l) | copy-start | bytes 6684676 | tf_op jit(solution)/shard_map/cond
  13.6 89.0 %copy-start.6 = (bf16[2,544,1024]{2,1,0:T(8,128)(2,1)S(1)}, bf16[2,544,1024]{2,1,0:T(8,128)(2,1)}, u32[]{:S(2)}) copy-start(bf16[2,544,1024]{2,1,0:T(8,128)(2,1)} %get-tuple-element.296.table_h) | copy-start | bytes 6684676 | tf_op jit(solution)/shard_map/cond
